TPU v7x, 32 devices: a whole 2x2x4 slice. The times are simulated.
32 devices in a mesh: parts: 2 (over x), wide: 16 (over z, y, core).
Axes of the slice: x: 2, y: 2, z: 4, core: 2. Of those that a mesh axis runs over, the one named last changes fastest.
Arguments:
- history: bfloat16 [2048, 8, 1024], P(('parts', 'wide')), parts along dimension 0, may hold values from -6 to 6
- pool: bfloat16 [512, 1024], P(('parts', 'wide')), parts along dimension 0, may hold values from -6 to 6
- cand_ids: int32 [64, 128], P(('parts', 'wide')), parts along dimension 0, may hold values from 0 to 255
- block_user: int32 [32, 64], P('parts'), parts along dimension 0, may hold values from 0 to 31, as said below
- norm_gain: float32 [1024], replicated, may hold values from 0.5 to 1.5
- w_in: bfloat16 [1024, 4096], replicated, may hold values from -0.1875 to 0.1875
- attn_gain: float32 [1024], replicated, may hold values from 0.25 to 1.75
- w_out: bfloat16 [1024, 1024], replicated, may hold values from -0.1875 to 0.1875
Outputs:
- scored: bfloat16 [64, 128, 1024], P(('parts', 'wide')), parts along dimension 0
There are 2 independent parts, one for each index of `parts`. A program takes and returns all parts, laid end to end along the dimension named above; an argument that names none is the same for every part. Nothing has to cross between parts.
Inputs may be any that keep to these rules, and one draw needn't show every extreme that they name: `block_user`: user u is ranked on device u // 2. At most 8 blocks of one owner belong to users ranked on one device; every draw reaches this, and some device receives 8 blocks from every owner.
All inputs are finite; a program needn't handle non-finite values.
Results may differ from a plain program's by a relative error of at most 0.0051.
Values may be sent and summed in bfloat16 or wider, within the bound.
A program may use at most 64 MiB of HBM per device.

v0:
```python
import jax
import jax.numpy as jnp
from jax import lax
from jax.sharding import PartitionSpec as P

HEADS = 8


def layer_norm(values, gain_vec):
    average = jnp.mean(values, axis=-1, keepdims=True)
    centered = values - average
    spread = jnp.mean(centered * centered, axis=-1, keepdims=True)
    return centered * lax.rsqrt(spread + 1e-05) * gain_vec


def project_cache(row_block, norm_gain, w_in):
    model_width = row_block.shape[-1]
    flat_rows = row_block.reshape(-1, model_width).astype(jnp.float32)
    normed = layer_norm(flat_rows, norm_gain).astype(jnp.bfloat16)
    front_proj = jnp.dot(normed, w_in[:, 2 * model_width :], preferred_element_type=jnp.float32)
    keyval = jax.nn.silu(front_proj).astype(jnp.bfloat16)
    return keyval.reshape(row_block.shape[:-1] + (2 * model_width,))


def body(history, pool, cand_ids, block_user, norm_gain, w_in, attn_gain, w_out):
    model_width = history.shape[2]
    block_rows = history.shape[1]
    owned = history.shape[0]
    head_size = model_width // HEADS
    devices = lax.axis_size("wide")
    device_id = lax.axis_index("wide")
    users_here = cand_ids.shape[0]
    per_user = cand_ids.shape[1]
    slot_count = max(1, 2 * owned // devices)
    target = block_user // users_here
    block_order = jnp.arange(owned, dtype=jnp.int32)
    shared = (target[:, :, None] == target[:, None, :]) & (
        block_order[None, None, :] < block_order[None, :, None]
    )
    within = jnp.sum(shared.astype(jnp.int32), axis=2)
    position_of = target * slot_count + within
    my_positions = lax.dynamic_index_in_dim(position_of, device_id, 0, keepdims=False)
    buffer_slots = jnp.arange(devices * slot_count, dtype=jnp.int32)
    matches = my_positions[None, :] == buffer_slots[:, None]
    source_block = jnp.sum(jnp.where(matches, block_order[None, :], 0), axis=1)
    filled = jnp.any(matches, axis=1)
    arrived = target == device_id
    slot_ids = jnp.arange(slot_count, dtype=jnp.int32)
    slot_match = arrived[:, None, :] & (within[:, None, :] == slot_ids[None, :, None])
    arrived_user = jnp.sum(jnp.where(slot_match, block_user[:, None, :] + 1, 0), axis=2) - 1
    owner_user = jnp.where(arrived_user >= 0, arrived_user - device_id * users_here, -1).reshape(-1)
    key_owner = jnp.repeat(owner_user, block_rows)
    outgoing = jnp.where(
        filled[:, None, None], jnp.take(history, source_block, axis=0), jnp.zeros((), history.dtype)
    )
    hidden_in = lax.all_to_all(outgoing, "wide", split_axis=0, concat_axis=0, tiled=True)
    keyval_in = project_cache(hidden_in, norm_gain, w_in)
    keys_flat = keyval_in.reshape(-1, 2 * model_width)
    wanted = cand_ids.reshape(-1)
    shard_rows = lax.all_gather(pool, "wide", axis=0, tiled=True)
    inside = (wanted >= 0) & (wanted < shard_rows.shape[0])
    found = jnp.take(shard_rows, jnp.clip(wanted, 0, shard_rows.shape[0] - 1), axis=0)
    item_rows = jnp.where(inside[:, None], found, jnp.zeros((), found.dtype))
    normed = layer_norm(item_rows.astype(jnp.float32), norm_gain).astype(jnp.bfloat16)
    front_proj = jnp.dot(normed, w_in[:, : 2 * model_width], preferred_element_type=jnp.float32)
    gate_up = jax.nn.silu(front_proj[:, :model_width])
    queries = jax.nn.silu(front_proj[:, model_width:]).astype(jnp.bfloat16)
    query_heads = queries.reshape(-1, HEADS, head_size)
    key_heads = keys_flat[:, :model_width].reshape(-1, HEADS, head_size)
    value_heads = keys_flat[:, model_width:].reshape(-1, HEADS, head_size)
    scores = jnp.einsum("rhd,khd->hrk", query_heads, key_heads, preferred_element_type=jnp.float32)
    row_user = jnp.repeat(jnp.arange(users_here, dtype=jnp.int32), per_user)
    same_user = row_user[:, None] == key_owner[None, :]
    weights = jnp.where(same_user[None], jax.nn.silu(scores * head_size ** (-0.5)), 0.0).astype(
        jnp.bfloat16
    )
    attended = jnp.einsum("hrk,khd->rhd", weights, value_heads, preferred_element_type=jnp.float32)
    attended = attended.reshape(-1, model_width)
    gated_rows = (layer_norm(attended, attn_gain) * gate_up).astype(jnp.bfloat16)
    result = jnp.dot(gated_rows, w_out, preferred_element_type=jnp.float32) + item_rows.astype(
        jnp.float32
    )
    return result.astype(jnp.bfloat16).reshape(users_here, per_user, model_width)


def solution(mesh):
    in_specs = (
        P(("parts", "wide"), None, None),
        P(("parts", "wide"), None),
        P(("parts", "wide"), None),
        P("parts", None),
        P(),
        P(),
        P(),
        P(),
    )
    out_specs = P(("parts", "wide"), None, None)
    return jax.shard_map(body, mesh=mesh, in_specs=in_specs, out_specs=out_specs, check_vma=False)
```

profile of v0, /device:TPU:9, one launch (start us, length us, event | category | flops | bytes accessed | tf_op | source)
XLA Modules:
  0.0 112.3 jit_solution(14735389463008998724)
XLA Ops:
  0.0 0.9 broadcast_compare_fusion.1
  0.9 0.5 convert_reduce_fusion.2
  1.4 0.1 select_reduce_fusion.1
  1.6 3.2 %gather_fusion = bf16[128,8,1024]{2,1,0:T(8,128)(2,1)} fusion(bf16[64,8,1024]{2,1,0:T(8,128)(2,1)} %param.8, s32[1024]{0:T(1024)S(1)} %pad_clamp_fusion.1), kind=kCustom, calls=%fused_computation | custom fusion | bytes 4194816 | tf_op jit(solution)/shard_map/jit(_take)/gather | solution.py:54
  4.9 3.0 %select_select_fusion = bf16[128,8,1024]{2,1,0:T(8,128)(2,1)} fusion(bf16[128,8,1024]{2,1,0:T(8,128)(2,1)} %gather_fusion, pred[128]{0:T(512)(128)(4,1)S(1)} %compare_and_fusion.1, pred[128]{0:T(512)(128)(4,1)S(1)} %fusion.45), kind=kLoop, calls=%fused_computation.25 | loop fusion | flops 2097152 | bytes 4194560 | tf_op jit(solution)/shard_map/jit(_where)/select_n | solution.py:53
  7.9 6.6 %all-to-all-start = ((bf16[128,8,1024]{2,1,0:T(8,128)(2,1)}), bf16[128,8,1024]{2,1,0:T(8,128)(2,1)}, u32[]{:S(2)}, u32[]{:S(2)}) async-start(bf16[128,8,1024]{2,1,0:T(8,128)(2,1)} %select_select_fusion), calls=%async_computation | async-start | bytes 4194304 | tf_op jit(solution)/shard_map/all_to_all | solution.py:56
  14.6 0.3 select_reduce_fusion
  15.1 0.1 eq.82
  15.3 58.8 %all_gather.3 = bf16[256,1024]{1,0:T(8,128)(2,1)S(1)} all-gather(bf16[16,1024]{1,0:T(8,128)(2,1)S(1)} %copy-done.2), channel_id=1, replica_groups=mesh['parts'=2,'wide'=16] {'wide'}, dimensions={0}, use_global_device_ids=true | all-gather | bytes 557056 | tf_op jit(solution)/shard_map/all_gather | solution.py:60
  74.1 1.2 %gather_fusion.1 = bf16[256,1024]{1,0:T(8,128)(2,1)S(1)} fusion(bf16[256,1024]{1,0:T(8,128)(2,1)S(1)} %all_gather.3, s32[1024]{0:T(1024)S(1)} %pad_clamp_fusion), kind=kCustom, calls=%fused_computation.1 | custom fusion | bytes 1049600 | tf_op jit(solution)/shard_map/jit(_take)/gather | solution.py:62
  75.3 0.3 convert_reduce_fusion.1
  75.6 0.3 fusion.26
  75.9 0.2 broadcast_compare_fusion
  76.2 0.3 copy-done.1
  76.4 4.9 %fusion.6 = f32[256,2048]{1,0:T(8,128)} fusion(bf16[1024,4096]{1,0:T(8,128)(2,1)} %param.13, bf16[256,1024]{1,0:T(8,128)(2,1)S(1)} %get-tuple-element.8, f32[1024]{0:T(1024)S(1)} %copy-done.5, f32[256]{0:T(256)S(1)} %add_rsqrt_fusion.2, f32[256]{0:T(256)S(1)} %broadcast_multiply_fusion.2), kind=kOutput, calls=%fused_computation.13 | convolution fusion | flops 1075052544 | bytes 6821888 | tf_op jit(solution)/shard_map/dot_general | solution.py:65
  81.3 1.9 %convert_reduce_fusion = f32[128,8]{1,0:T(8,128)S(1)} fusion(bf16[128,8,1024]{2,1,0:T(8,128)(2,1)} %all-to-all-done), kind=kLoop, calls=%fused_computation.5 | loop fusion | flops 2096128 | bytes 2101248 | tf_op jit(solution)/shard_map/reduce_sum | solution.py:10
  83.4 2.3 %fusion.5 = f32[128,8]{1,0:T(8,128)S(1)} fusion(bf16[128,8,1024]{2,1,0:T(8,128)(2,1)} %all-to-all-done, f32[128,8]{1,0:T(8,128)S(1)} %broadcast_multiply_fusion), kind=kLoop, calls=%fused_computation.12 | loop fusion | flops 4193280 | bytes 2105344 | tf_op jit(solution)/shard_map/reduce_sum | solution.py:12
  85.8 8.1 %multiply_convert_fusion = bf16[1024,2048]{1,0:T(8,128)(2,1)S(1)} fusion(bf16[1024,4096]{1,0:T(8,128)(2,1)} %param.13, bf16[128,8,1024]{2,1,0:T(8,128)(2,1)} %all-to-all-done, f32[1024]{0:T(1024)S(1)} %copy-done.5, f32[1024]{0:T(1024)S(1)} %rsqrt.28, f32[1024]{0:T(1024)S(1)} %div.49), kind=kOutput, calls=%fused_computation.3 | convolution fusion | flops 4310695936 | bytes 10498048 | tf_op jit(solution)/shard_map/dot_general | solution.py:20
  93.9 2.7 %slice_bitcast_fusion = (bf16[128,8,8,128]{3,2,1,0:T(8,128)(2,1)}, bf16[1024,1024]{1,0:T(8,128)(2,1)}) fusion(bf16[1024,2048]{1,0:T(8,128)(2,1)S(1)} %multiply_convert_fusion), kind=kLoop, calls=%fused_computation.21 | loop fusion | bytes 8388608
  96.6 4.0 %copy.21 = bf16[1024,1024]{0,1:T(8,128)(2,1)} copy(bf16[1024,1024]{1,0:T(8,128)(2,1)} %get-tuple-element.10) | data formatting | bytes 4194304 | tf_op jit(solution)/shard_map/reshape | solution.py:70
  100.6 6.9 %fusion.54 = (f32[256]{0:T(256)S(1)}, f32[8,128,256]{2,1,0:T(8,128)S(1)}) fusion(bf16[1024,8,128]{0,2,1:T(8,128)(2,1)} %bitcast.57, pred[256,1024]{1,0:T(8,128)(4,1)S(1)} %broadcast_compare_fusion, bf16[128,8,8,128]{3,2,1,0:T(8,128)(2,1)} %get-tuple-element.9, f32[256,2048]{1,0:T(8,128)} %fusion.6), kind=kOutput, calls=%fused_computation.95 | convolution fusion | flops 1089994496 | bytes 6554624 | tf_op jit(solution)/shard_map/hrk,khd->rhd/dot_general | solution.py:77
  107.5 0.2 fusion.30
  107.7 1.3 %copy.22 = f32[256,1024]{1,0:T(8,128)} copy(f32[256,1024]{0,1:T(8,128)S(1)} %bitcast.56) | data formatting | bytes 2097152 | tf_op jit(solution)/shard_map/reshape | solution.py:78
  109.0 3.3 %fusion.23 = bf16[256,1024]{1,0:T(8,128)(2,1)} fusion(bf16[256,1024]{1,0:T(8,128)(2,1)} %copy-done.1, bf16[1024,1024]{1,0:T(8,128)(2,1)S(1)} %copy-done, f32[256,2048]{1,0:T(8,128)} %fusion.6, f32[256,1024]{1,0:T(8,128)} %copy.22, f32[1024]{0:T(1024)S(1)} %copy-done.6, f32[256]{0:T(256)S(1)} %add_rsqrt_fusion.1, f32[256]{0:T(256)S(1)} %broadcast_multiply_fusion.1), kind=kOutput, calls=%fused_computation.29 | convolution fusion | flops 540016640 | bytes 5249024 | tf_op jit(solution)/shard_map/dot_general | solution.py:80
  (38 shorter events, 0.6 us)
Async XLA Ops:
  0.0 109.0 %copy-start = (bf16[1024,1024]{1,0:T(8,128)(2,1)S(1)}, bf16[1024,1024]{1,0:T(8,128)(2,1)}, u32[]{:S(2)}) copy-start(bf16[1024,1024]{1,0:T(8,128)(2,1)} %param.15) | copy-start | bytes 6291460
  4.9 9.7 %copy-start.3 = (s32[16,64]{1,0:T(8,128)S(1)}, s32[16,64]{1,0:T(8,128)}, u32[]{:S(2)}) copy-start(s32[16,64]{1,0:T(8,128)} %param.11) | copy-start | bytes 12292
  4.9 10.3 %copy-start.4 = (s32[2,128]{1,0:T(2,128)S(1)}, s32[2,128]{1,0:T(2,128)}, u32[]{:S(2)}) copy-start(s32[2,128]{1,0:T(2,128)} %param.10) | copy-start | bytes 3076
  4.9 10.4 %copy-start.2 = (bf16[16,1024]{1,0:T(8,128)(2,1)S(1)}, bf16[16,1024]{1,0:T(8,128)(2,1)}, u32[]{:S(2)}) copy-start(bf16[16,1024]{1,0:T(8,128)(2,1)} %param.9) | copy-start | bytes 98308
  7.9 73.4 %all-to-all-start = ((bf16[128,8,1024]{2,1,0:T(8,128)(2,1)}), bf16[128,8,1024]{2,1,0:T(8,128)(2,1)}, u32[]{:S(2)}, u32[]{:S(2)}) async-start(bf16[128,8,1024]{2,1,0:T(8,128)(2,1)} %select_select_fusion), calls=%async_computation | async-start | bytes 4194304 | tf_op jit(solution)/shard_map/all_to_all | solution.py:56
  14.5 61.9 %copy-start.5 = (f32[1024]{0:T(1024)S(1)}, f32[1024]{0:T(1024)}, u32[]{:S(2)}) copy-start(f32[1024]{0:T(1024)} %param.12) | copy-start | bytes 12292
  75.6 0.8 copy-start.1
  100.6 8.4 %copy-start.6 = (f32[1024]{0:T(1024)S(1)}, f32[1024]{0:T(1024)}, u32[]{:S(2)}) copy-start(f32[1024]{0:T(1024)} %param.14) | copy-start | bytes 12292
where the time goes:
time: 113 us; the launch traced here: 112 us
  blocking collectives  58.8 us (52%)
  matrix products  23.3 us (21%)
  local copies, waits for them, and re-layouts  13.1 us (12%)
  other arithmetic  10.3 us (9%)
  starting transfers between devices  6.61 us (6%)
    all_gather x1, blocking collectives, body(): shard_rows = lax.all_gather(pool, 'wide', axis=0, tiled=True)  58.8 us
    dot_general x1, matrix products, project_cache(): jnp.dot(normed, w_in[:, 2 * model_width:], preferred_element_type=jnp.flo...  8.12 us
    dot_general x1, matrix products, body(): jnp.einsum('hrk,khd->rhd', weights, value_heads, preferred_element_type=j...  6.91 us
    all_to_all x1, starting transfers between devices, body(): lax.all_to_all(outgoing, 'wide', split_axis=0, concat_axis=0, tiled=True)  6.61 us
    dot_general x1, matrix products, body(): jnp.dot(normed, w_in[:, :2 * model_width], preferred_element_type=jnp.flo...  4.9 us
    reshape x1, local copies, waits for them, and re-layouts, body(): value_heads = keys_flat[:, model_width:].reshape(-1, HEADS, head_size)  3.95 us
    dot_general x1, matrix products, body(): jnp.dot(gated_rows, w_out, preferred_element_type=jnp.float32)  3.33 us
    gather x1, local copies, waits for them, and re-layouts, body(): jnp.take(history, source_block, axis=0)  3.24 us
  transfers between devices with their start and end apart: 1, of which 0 were waited for; matrix products, arithmetic and copies ran while one was open for 7% of the time, Pallas kernels for 0%

commit v1 on v0

v1 whole, which is shorter than its diff:
```python
import functools

import jax
import jax.numpy as jnp
from jax import lax
from jax.experimental import pallas as pl
from jax.experimental.pallas import tpu as pltpu
from jax.sharding import PartitionSpec as P

HEADS = 8
GROUPS = 4
F32 = jnp.float32
BF16 = jnp.bfloat16


def silu(x):
    half = 0.5 * x
    return half + half * jnp.tanh(half)


def normalize(values):
    average = jnp.mean(values, axis=-1, keepdims=True)
    centered = values - average
    spread = jnp.mean(centered * centered, axis=-1, keepdims=True)
    return centered * lax.rsqrt(spread + 1e-05)


def flip(me, step, bits):
    total = 0
    for k in range(bits):
        total = total + (1 << k) * lax.rem(me // (1 << k) + step // (1 << k), 2)
    return total


def kernel(
    n, per_user,
    hist_hbm, pool_ref, ids_ref, pos_ref, owner_ref, gain_ref, again_ref, win_hbm, wout_hbm,
    out_ref,
    hist, win, wout, sendb, recvb, poolb, queries, gate, items, normed, acc,
    local_sem, send_sem, recv_sem, pool_send, pool_recv,
):
    bits = (n - 1).bit_length()
    me = lax.axis_index("wide")
    width = hist.shape[1]
    head = width // HEADS
    pair_rows = sendb.shape[1]
    group = n // GROUPS
    rows = group * pair_rows

    local = [
        pltpu.make_async_copy(hist_hbm, hist, local_sem.at[0]),
        pltpu.make_async_copy(win_hbm, win, local_sem.at[1]),
        pltpu.make_async_copy(wout_hbm, wout, local_sem.at[2]),
    ]
    for copy in local:
        copy.start()

    barrier = pltpu.get_barrier_semaphore()

    def greet(step, carry):
        pl.semaphore_signal(
            barrier, inc=1, device_id={"wide": flip(me, step, bits)},
            device_id_type=pl.DeviceIdType.MESH,
        )
        return carry

    lax.fori_loop(1, n, greet, 0)
    poolb[0] = pool_ref[...]

    def block_copy(step):
        return pltpu.make_async_remote_copy(
            src_ref=sendb.at[step], dst_ref=recvb.at[step],
            send_sem=send_sem.at[step], recv_sem=recv_sem.at[step],
            device_id={"wide": flip(me, step, bits)}, device_id_type=pl.DeviceIdType.MESH,
        )

    def pool_copy(stage):
        count = 1 << stage
        return pltpu.make_async_remote_copy(
            src_ref=poolb.at[pl.ds(0, count)], dst_ref=poolb.at[pl.ds(count, count)],
            send_sem=pool_send.at[stage], recv_sem=pool_recv.at[stage],
            device_id={"wide": flip(me, 1 << (bits - 1 - stage), bits)},
            device_id_type=pl.DeviceIdType.MESH,
        )

    def pick(g):
        wanted = lax.broadcasted_iota(jnp.int32, (rows, hist.shape[0]), 0) + g * rows
        chosen = (wanted == pos_ref[...]).astype(F32).astype(BF16)
        found = jnp.dot(chosen, hist[...], preferred_element_type=F32)
        found = found.reshape(group, pair_rows, width).astype(BF16)
        sendb[pl.ds(g * group, group)] = found
        if g == 0:
            recvb[pl.ds(0, 1)] = found[:1]

    def send(g):
        def one(i, carry):
            block_copy((g + 1) * group - 1 - i).start()
            return carry

        lax.fori_loop(0, group if g else group - 1, one, 0)

    local[0].wait()
    pick(GROUPS - 1)
    pl.semaphore_wait(barrier, n - 1)
    pool_copy(0).start()
    for g in reversed(range(GROUPS)):
        send(g)
        if g:
            pick(g - 1)
    for stage in range(bits):
        if stage:
            pool_copy(stage).start()
        pool_copy(stage).wait_recv()

    shards, shard_rows, _ = poolb.shape
    pool_rows = shards * shard_rows
    lanes = lax.broadcasted_iota(jnp.int32, (ids_ref.shape[0], pool_rows), 1)
    chosen = (lanes == ids_ref[...]).astype(F32).astype(BF16)
    table = poolb[...].astype(F32).reshape(pool_rows, width).astype(BF16)
    found = jnp.dot(chosen, table, preferred_element_type=F32)
    items[...] = found.astype(BF16)
    normed_items = (normalize(found) * gain_ref[...]).astype(BF16)
    local[1].wait()
    local[2].wait()
    wide_cols = 2 * head

    def front(j, carry):
        cols = pl.ds(pl.multiple_of(j * wide_cols, wide_cols), wide_cols)
        gate[:, cols] = silu(jnp.dot(normed_items, win[:, cols], preferred_element_type=F32))
        qcols = pl.ds(pl.multiple_of(j * wide_cols + width, wide_cols), wide_cols)
        queries[:, cols] = silu(
            jnp.dot(normed_items, win[:, qcols], preferred_element_type=F32)
        ).astype(BF16)
        return carry

    lax.fori_loop(0, HEADS // 2, front, 0)
    acc[...] = jnp.zeros_like(acc)
    row_user = lax.broadcasted_iota(jnp.int32, (acc.shape[0], rows), 0) // per_user

    for g in range(GROUPS):
        def arrive(step, carry):
            block_copy(step).wait_recv()
            return carry

        lax.fori_loop(max(1, g * group), (g + 1) * group, arrive, 0)
        hidden = recvb[pl.ds(g * group, group)].astype(F32).reshape(rows, width)
        normed[...] = (normalize(hidden) * gain_ref[...]).astype(BF16)
        mask = row_user == owner_ref[:, g * rows:(g + 1) * rows]

        def heads(j, carry):
            cols = pl.ds(pl.multiple_of(j * wide_cols, wide_cols), wide_cols)
            kcols = pl.ds(pl.multiple_of(j * wide_cols + 2 * width, wide_cols), wide_cols)
            vcols = pl.ds(pl.multiple_of(j * wide_cols + 3 * width, wide_cols), wide_cols)
            keys = silu(jnp.dot(normed[...], win[:, kcols], preferred_element_type=F32)).astype(BF16)
            vals = silu(jnp.dot(normed[...], win[:, vcols], preferred_element_type=F32)).astype(BF16)
            query = queries[:, cols]
            parts = []
            for h in range(2):
                part = slice(h * head, (h + 1) * head)
                scores = lax.dot_general(
                    query[:, part], keys[:, part], (((1,), (1,)), ((), ())),
                    preferred_element_type=F32,
                )
                weights = jnp.where(mask, silu(scores * head ** (-0.5)), 0.0).astype(BF16)
                parts.append(jnp.dot(weights, vals[:, part], preferred_element_type=F32))
            acc[:, cols] += jnp.concatenate(parts, axis=1)
            return carry

        lax.fori_loop(0, HEADS // 2, heads, 0)

    gated = (normalize(acc[...]) * again_ref[...] * gate[...]).astype(BF16)

    def last(j, carry):
        cols = pl.ds(pl.multiple_of(j * wide_cols, wide_cols), wide_cols)
        total = jnp.dot(gated, wout[:, cols], preferred_element_type=F32)
        out_ref[:, cols] = (total + items[:, cols].astype(F32)).astype(BF16)
        return carry

    lax.fori_loop(0, HEADS // 2, last, 0)

    for stage in range(bits):
        pool_copy(stage).wait_send()

    def sent(step, carry):
        block_copy(step).wait_send()
        return carry

    lax.fori_loop(1, n, sent, 0)


def body(n, history, pool, cand_ids, block_user, norm_gain, w_in, attn_gain, w_out):
    owned, block_rows, width = history.shape
    users_here, per_user = cand_ids.shape
    slot_count = max(1, 2 * owned // n)
    pair_rows = slot_count * block_rows
    bits = (n - 1).bit_length()
    me = lax.axis_index("wide")

    target = block_user // users_here
    order = jnp.arange(owned, dtype=jnp.int32)
    shared = (target[:, :, None] == target[:, None, :]) & (order[None, None, :] < order[None, :, None])
    within = jnp.sum(shared.astype(jnp.int32), axis=2)
    mine_target = lax.dynamic_index_in_dim(target, me, 0, keepdims=True)
    mine_within = lax.dynamic_index_in_dim(within, me, 0, keepdims=True)
    pos = (mine_target ^ me) * slot_count + mine_within
    pos = (pos[:, :, None] * block_rows + jnp.arange(block_rows, dtype=jnp.int32)).reshape(1, -1)
    owner = jnp.arange(n, dtype=jnp.int32)[:, None] ^ me
    slot = jnp.where(target == me, owner * slot_count + within, -1).reshape(-1, 1)
    label = (block_user - me * users_here + 1).reshape(-1, 1)
    event_slot = jnp.arange(n * pair_rows, dtype=jnp.int32)[None, :] // block_rows
    key_owner = jnp.sum(jnp.where(slot == event_slot, label, 0), axis=0, keepdims=True) - 1

    ids = cand_ids.reshape(-1, 1)
    shard_rows = pool.shape[0]
    relative = (ids // shard_rows) ^ me
    place = jnp.zeros_like(relative)
    for k in range(bits):
        place = place + (((relative >> k) & 1) << (bits - 1 - k))
    ids = place * shard_rows + ids % shard_rows

    cands = users_here * per_user
    vmem = pl.BlockSpec(memory_space=pltpu.VMEM)
    hbm = pl.BlockSpec(memory_space=pl.ANY)
    out = pl.pallas_call(
        functools.partial(kernel, n, per_user),
        out_shape=jax.ShapeDtypeStruct((cands, width), BF16),
        in_specs=[hbm, vmem, vmem, vmem, vmem, vmem, vmem, hbm, hbm],
        out_specs=vmem,
        scratch_shapes=[
            pltpu.VMEM((owned * block_rows, width), BF16),
            pltpu.VMEM(w_in.shape, BF16),
            pltpu.VMEM(w_out.shape, BF16),
            pltpu.VMEM((n, pair_rows, width), BF16),
            pltpu.VMEM((n, pair_rows, width), BF16),
            pltpu.VMEM((n, shard_rows, width), BF16),
            pltpu.VMEM((cands, width), BF16),
            pltpu.VMEM((cands, width), F32),
            pltpu.VMEM((cands, width), BF16),
            pltpu.VMEM((n // GROUPS * pair_rows, width), BF16),
            pltpu.VMEM((cands, width), F32),
            pltpu.SemaphoreType.DMA((3,)),
            pltpu.SemaphoreType.DMA((n,)),
            pltpu.SemaphoreType.DMA((n,)),
            pltpu.SemaphoreType.DMA((bits,)),
            pltpu.SemaphoreType.DMA((bits,)),
        ],
        compiler_params=pltpu.CompilerParams(
            collective_id=0, has_side_effects=True, vmem_limit_bytes=50 * 1024 * 1024
        ),
    )(
        history.reshape(-1, width), pool, ids, pos, key_owner, norm_gain.reshape(1, -1),
        attn_gain.reshape(1, -1), w_in, w_out,
    )
    return out.reshape(users_here, per_user, width)


def solution(mesh):
    in_specs = (
        P(("parts", "wide"), None, None),
        P(("parts", "wide"), None),
        P(("parts", "wide"), None),
        P("parts", None),
        P(),
        P(),
        P(),
        P(),
    )
    out_specs = P(("parts", "wide"), None, None)
    return jax.shard_map(
        functools.partial(body, mesh.shape["wide"]), mesh=mesh, in_specs=in_specs,
        out_specs=out_specs, check_vma=False,
    )
```

time: 113 us -> 83.1 us (0.74)
  the two profiles are of different devices: /device:TPU:9 before, /device:TPU:13 now
where the time goes in v1:
time: 83.1 us; the launch traced here: 82.7 us
  Pallas kernels  72.8 us (88%)
  local copies, waits for them, and re-layouts  6.95 us (8%)
  other arithmetic  2.87 us (3%)
    pallas_call x1, Pallas kernels, body(): pl.pallas_call(functools.partial(kernel, n, per_user), out_shape=jax.Shap...  72.8 us
    unnamed x11, local copies, waits for them, and re-layouts  5.74 us

profile of v1, /device:TPU:13, one launch (start us, length us, event | category | flops | bytes accessed | tf_op | source)
XLA Modules:
  0.0 82.7 jit_solution(5312439457077792287)
XLA Ops:
  0.0 0.7 add_select_fusion.2
  0.7 0.5 convert_reduce_fusion
  1.3 0.8 add_select_fusion.3
  2.0 0.1 eq.41
  2.1 0.1 broadcast_in_dim.12
  2.2 0.6 select_reduce_fusion
  2.9 0.1 add.129
  2.9 0.1 add.130
  3.0 0.1 add.132
  3.1 0.8 copy.17
  3.9 0.2 fusion.1.ids_ref
  4.1 0.0 copy-start
  4.2 1.6 %copy-done = bf16[1024,1024]{1,0:T(8,128)(2,1)S(1)} copy-done((bf16[1024,1024]{1,0:T(8,128)(2,1)S(1)}, bf16[1024,1024]{1,0:T(8,128)(2,1)}, u32[]{:S(2)}) %copy-start) | copy-done | bytes 2097176
  5.7 0.0 copy-start.1
  5.7 1.2 %copy-done.1 = bf16[64,8,1024]{2,1,0:T(8,128)(2,1)S(1)} copy-done((bf16[64,8,1024]{2,1,0:T(8,128)(2,1)S(1)}, bf16[64,8,1024]{2,1,0:T(8,128)(2,1)}, u32[]{:S(2)}) %copy-start.1) | copy-done | bytes 1048600
  7.0 0.0 copy-start.2
  7.0 0.8 copy-done.2
  7.7 0.0 copy-start.3
  7.7 0.7 copy-done.3
  8.4 0.0 copy-start.4
  8.4 0.7 copy-done.4
  9.1 72.8 %shard_map.82 = bf16[256,1024]{1,0:T(8,128)(2,1)S(1)} custom-call(bf16[512,1024]{1,0:T(8,128)(2,1)S(1)} %bitcast.11, bf16[16,1024]{1,0:T(8,128)(2,1)S(1)} %copy-done.2, s32[256,1]{1,0:T(8,128)S(1)} %fusion.1.ids_ref, s32[1,512]{1,0:T(1,128)S(1)} %add.133.pos_ref, s32[1,1024]{1,0:T(1,128)S(1)} %bitcast.12, f32[1,1024]{1,0:T(1,128)S(1)} %bitcast.13, ...), custom_call_target="tpu_custom_call" | custom-call | tf_op jit(solution)/shard_map/pallas_call | solution.py:224
  81.9 0.8 copy.27
  (7 shorter events, 0.1 us)
Async XLA Ops:
  4.1 1.6 %copy-start = (bf16[1024,1024]{1,0:T(8,128)(2,1)S(1)}, bf16[1024,1024]{1,0:T(8,128)(2,1)}, u32[]{:S(2)}) copy-start(bf16[1024,1024]{1,0:T(8,128)(2,1)} %wout_hbm.1) | copy-start | bytes 6291460
  5.7 1.2 %copy-start.1 = (bf16[64,8,1024]{2,1,0:T(8,128)(2,1)S(1)}, bf16[64,8,1024]{2,1,0:T(8,128)(2,1)}, u32[]{:S(2)}) copy-start(bf16[64,8,1024]{2,1,0:T(8,128)(2,1)} %param.8) | copy-start | bytes 3145732
  7.0 0.8 copy-start.2
  7.7 0.7 copy-start.3
  8.4 0.7 copy-start.4

commit v2 on v1

v2 whole, which is shorter than its diff:
```python
import functools

import jax
import jax.numpy as jnp
from jax import lax
from jax.experimental import pallas as pl
from jax.experimental.pallas import tpu as pltpu
from jax.sharding import PartitionSpec as P

HEADS = 8
F32 = jnp.float32
BF16 = jnp.bfloat16


def silu(x):
    half = 0.5 * x
    return half + half * jnp.tanh(half)


def normalize(values):
    average = jnp.mean(values, axis=-1, keepdims=True)
    centered = values - average
    spread = jnp.mean(centered * centered, axis=-1, keepdims=True)
    return centered * lax.rsqrt(spread + 1e-05)


def flip(me, step, bits):
    total = 0
    for k in range(bits):
        total = total + (1 << k) * ((me // (1 << k) + step // (1 << k)) % 2)
    return total


def lane(shape):
    return lax.broadcasted_iota(jnp.int32, shape, len(shape) - 1)


def row(shape):
    return lax.broadcasted_iota(jnp.int32, shape, 0)


def exact_dot(a, b):
    return jnp.dot(a, b, preferred_element_type=F32, precision=lax.Precision.HIGHEST)


def kernel(
    n, users_here, per_user, block_rows,
    hist_hbm, pool_hbm, ids_hbm, user_hbm, gain_hbm, again_hbm, win_hbm, wout_hbm,
    out_ref,
    hist, win, wout, gain, again, ids, block_user, sendb, recvb, poolb,
    queries, mate_queries, gate, items, normed, acc, part_out, part_in,
    local_sem, send_sem, recv_sem, pool_send, pool_recv, part_send, part_recv, ids_sem,
):
    bits = (n - 1).bit_length()
    half, quarter = n // 2, n // 4
    me = lax.axis_index("wide")
    middle = (me // half + me // quarter) % 2
    is_middle = middle == 1
    mate = flip(me, half + quarter, bits)
    owned_rows, width = hist.shape
    owned = owned_rows // block_rows
    head = width // HEADS
    wide_cols = 2 * head
    pair_rows = sendb.shape[1]
    slots = pair_rows // block_rows
    cands = acc.shape[0]
    mesh_id = pl.DeviceIdType.MESH

    sources = (user_hbm, hist_hbm, pool_hbm, ids_hbm, gain_hbm, again_hbm, win_hbm, wout_hbm)
    places = (block_user, hist, poolb.at[0], ids.at[0], gain, again, win, wout)
    local = [
        pltpu.make_async_copy(source, place, local_sem.at[i])
        for i, (source, place) in enumerate(zip(sources, places))
    ]
    for copy in local:
        copy.start()

    barrier = pltpu.get_barrier_semaphore()

    def greet(step, carry):
        pl.semaphore_signal(
            barrier, inc=1, device_id={"wide": flip(me, step, bits)}, device_id_type=mesh_id
        )
        return carry

    lax.fori_loop(1, n, greet, 0)

    def block_copy(step, peer, slot):
        return pltpu.make_async_remote_copy(
            src_ref=sendb.at[step], dst_ref=recvb.at[slot],
            send_sem=send_sem.at[step], recv_sem=recv_sem.at[slot],
            device_id={"wide": flip(me, peer, bits)}, device_id_type=mesh_id,
        )

    def pool_copy(stage):
        count = 1 << stage
        return pltpu.make_async_remote_copy(
            src_ref=poolb.at[pl.ds(0, count)], dst_ref=poolb.at[pl.ds(count, count)],
            send_sem=pool_send.at[stage], recv_sem=pool_recv.at[stage],
            device_id={"wide": flip(me, 1 << (bits - 1 - stage), bits)}, device_id_type=mesh_id,
        )

    ids_copy = pltpu.make_async_remote_copy(
        src_ref=ids.at[0], dst_ref=ids.at[1], send_sem=ids_sem.at[0], recv_sem=ids_sem.at[1],
        device_id={"wide": mate}, device_id_type=mesh_id,
    )

    def part_copy(j):
        return pltpu.make_async_remote_copy(
            src_ref=part_out.at[j], dst_ref=part_in.at[j],
            send_sem=part_send.at[j], recv_sem=part_recv.at[j],
            device_id={"wide": mate}, device_id_type=mesh_id,
        )

    local[0].wait()
    users = block_user[...]
    targets = users // users_here
    mine = jnp.sum(jnp.where(row((n, owned)) == me, targets, 0), axis=0, keepdims=True)
    square = (owned, owned)
    mine_down = jnp.sum(jnp.where(row(square) == lane(square), mine, 0), axis=1, keepdims=True)
    earlier = row(square) < lane(square)
    within = jnp.sum(
        jnp.where((mine_down == mine) & earlier, 1, 0), axis=0, keepdims=True
    )
    position = flip(me, mine, bits) * slots + within
    spread_shape = (owned, owned_rows)
    spread = jnp.where(lane(spread_shape) // block_rows == row(spread_shape), 1.0, 0.0)
    position = exact_dot(jnp.broadcast_to(position.astype(F32), (8, owned)), spread)[:1]
    position = position.astype(jnp.int32) * block_rows + lane((1, owned_rows)) % block_rows
    for copy in local[1:4]:
        copy.wait()

    def pick(first, count):
        wanted = row((count * pair_rows, owned_rows)) + first * pair_rows
        chosen = jnp.where(wanted == position, 1.0, 0.0).astype(BF16)
        found = jnp.dot(chosen, hist[...], preferred_element_type=F32)
        sendb[pl.ds(first, count)] = found.reshape(count, pair_rows, width).astype(BF16)

    def send_all(first, last, peer_shift, slot_shift):
        def one(i, carry):
            step = last - 1 - i
            block_copy(step, step - peer_shift, step + slot_shift).start()
            return carry

        lax.fori_loop(0, last - first, one, 0)

    pl.semaphore_wait(barrier, n - 1)
    pool_copy(0).start()
    ids_copy.start()
    pick(half + quarter, quarter)
    pool_copy(0).wait_recv()
    pool_copy(1).start()
    pick(half, quarter)
    pool_copy(1).wait_recv()
    pool_copy(2).start()

    @pl.when(is_middle)
    def _():
        recvb[pl.ds(half, 1)] = sendb[pl.ds(half + quarter, 1)]
        send_all(half + quarter + 1, n, half + quarter, -quarter)
        send_all(half, half + quarter, 0, 0)

    @pl.when(jnp.logical_not(is_middle))
    def _():
        send_all(half, half + quarter, quarter, quarter)
        send_all(half + quarter, n, 0, 0)

    pick(quarter, quarter)
    for stage in range(3, bits):
        pool_copy(stage - 1).wait_recv()
        pool_copy(stage).start()
    pick(0, quarter)
    send_all(1, half, 0, 0)
    recvb[pl.ds(0, 1)] = sendb[pl.ds(0, 1)]
    pool_copy(bits - 1).wait_recv()

    def event_users(ranker, first, flips_from):
        shape = (n, half * pair_rows)
        arrived = targets == ranker
        count = exact_dot(jnp.where(arrived, 1.0, 0.0), jnp.where(earlier, 1.0, 0.0))
        count = count.astype(jnp.int32)
        label = users - ranker * users_here + 1
        lanes = lane(shape)
        slot_here = (lanes % pair_rows) // block_rows
        owner = flip(me, lane((1, half * pair_rows)) // pair_rows + flips_from, bits)
        total = jnp.zeros(shape, jnp.int32)
        for slot in range(slots):
            at_slot = jnp.sum(
                jnp.where(arrived & (count == slot), label, 0), axis=1, keepdims=True
            )
            total = total + jnp.where(slot_here == slot, at_slot, 0)
        return jnp.sum(jnp.where(row(shape) == owner, total, 0), axis=0, keepdims=True) - 1

    near_users = event_users(me, 0, 0)
    far_users = event_users(jnp.where(is_middle, mate, me), half, half * (1 - middle))

    shards, shard_rows, _ = poolb.shape
    pool_rows = shards * shard_rows
    for copy in local[4:]:
        copy.wait()

    def pool_items(which):
        wanted = ids[which]
        relative = flip(me, wanted // shard_rows, bits)
        place = jnp.zeros_like(relative)
        for k in range(bits):
            place = place + ((relative // (1 << k)) % 2) * (1 << (bits - 1 - k))
        place = place * shard_rows + wanted % shard_rows
        table = poolb[...].astype(F32).reshape(pool_rows, width).astype(BF16)
        found = []
        for u in range(users_here):
            chosen = jnp.where(row((pool_rows, per_user)) == place[u:u + 1], 1.0, 0.0).astype(BF16)
            found.append(lax.dot_general(
                chosen, table, (((0,), (0,)), ((), ())), preferred_element_type=F32
            ))
        found = jnp.concatenate(found, axis=0)
        return found, (normalize(found) * gain[...]).astype(BF16)

    def columns(j, offset=0):
        return pl.ds(pl.multiple_of(j * wide_cols + offset, wide_cols), wide_cols)

    def project(rows_in, j, offset):
        return silu(jnp.dot(rows_in, win[:, columns(j, offset)], preferred_element_type=F32))

    def each_pair(step):
        def one(j, carry):
            step(j)
            return carry

        lax.fori_loop(0, HEADS // 2, one, 0)

    def attend(first, count, query_ref, event_user, emit):
        rows = count * pair_rows
        hidden = recvb[pl.ds(first, count)].astype(F32).reshape(rows, width)
        normed[pl.ds(0, rows)] = (normalize(hidden) * gain[...]).astype(BF16)
        mask = row((cands, rows)) // per_user == event_user

        def pair(j):
            here = normed[pl.ds(0, rows)]
            keys = project(here, j, 2 * width).astype(BF16)
            vals = project(here, j, 3 * width).astype(BF16)
            query = query_ref[:, columns(j)]
            parts = []
            for h in range(2):
                part = slice(h * head, (h + 1) * head)
                scores = lax.dot_general(
                    query[:, part], keys[:, part], (((1,), (1,)), ((), ())),
                    preferred_element_type=F32,
                )
                weights = jnp.where(mask, silu(scores * head ** (-0.5)), 0.0).astype(BF16)
                parts.append(jnp.dot(weights, vals[:, part], preferred_element_type=F32))
            emit(j, jnp.concatenate(parts, axis=1))

        each_pair(pair)

    def arrive(first, last):
        def one(slot, carry):
            block_copy(slot, slot, slot).wait_recv()
            return carry

        lax.fori_loop(first, last, one, 0)

    def add(j, value):
        acc[:, columns(j)] += value

    ids_copy.wait_recv()

    @pl.when(is_middle)
    def _():
        _, mate_items = pool_items(1)

        def ask(j):
            mate_queries[:, columns(j)] = project(mate_items, j, width).astype(BF16)

        each_pair(ask)
        arrive(half + 1, n)

        def emit(j, value):
            part_out[j] = value.astype(BF16)
            part_copy(j).start()

        attend(half, half, mate_queries, far_users, emit)

    found, normed_items = pool_items(0)
    items[...] = found.astype(BF16)

    def front(j):
        gate[:, columns(j)] = project(normed_items, j, 0)
        queries[:, columns(j)] = project(normed_items, j, width).astype(BF16)

    each_pair(front)
    acc[...] = jnp.zeros_like(acc)
    arrive(1, half)
    attend(0, half, queries, near_users, add)

    @pl.when(is_middle)
    def _():
        def join(j):
            part_copy(j).wait_recv()
            add(j, part_in[j].astype(F32))

        each_pair(join)

    @pl.when(jnp.logical_not(is_middle))
    def _():
        for g in range(2):
            first = half + g * quarter
            arrive(first, first + quarter)
            event_user = far_users[:, g * quarter * pair_rows:(g + 1) * quarter * pair_rows]
            attend(first, quarter, queries, event_user, add)

    gated = (normalize(acc[...]) * again[...] * gate[...]).astype(BF16)

    def last(j):
        total = jnp.dot(gated, wout[:, columns(j)], preferred_element_type=F32)
        out_ref[:, columns(j)] = (total + items[:, columns(j)].astype(F32)).astype(BF16)

    each_pair(last)

    ids_copy.wait_send()
    for stage in range(bits):
        pool_copy(stage).wait_send()

    def sent(step, carry):
        block_copy(step, 1, step).wait_send()
        return carry

    lax.fori_loop(1, half + quarter, sent, 0)
    lax.fori_loop(half + quarter + 1, n, sent, 0)

    @pl.when(jnp.logical_not(is_middle))
    def _():
        sent(half + quarter, 0)

    @pl.when(is_middle)
    def _():
        each_pair(lambda j: part_copy(j).wait_send())


def body(n, history, pool, cand_ids, block_user, norm_gain, w_in, attn_gain, w_out):
    owned, block_rows, width = history.shape
    users_here, per_user = cand_ids.shape
    slot_count = max(1, 2 * owned // n)
    pair_rows = slot_count * block_rows
    shard_rows = pool.shape[0]
    bits = (n - 1).bit_length()
    cands = users_here * per_user
    pairs = (HEADS // 2, cands, 2 * width // HEADS)
    hbm = pl.BlockSpec(memory_space=pl.ANY)
    dma = pltpu.SemaphoreType.DMA
    out = pl.pallas_call(
        functools.partial(kernel, n, users_here, per_user, block_rows),
        out_shape=jax.ShapeDtypeStruct((cands, width), BF16),
        in_specs=[hbm] * 8,
        out_specs=pl.BlockSpec(memory_space=pltpu.VMEM),
        scratch_shapes=[
            pltpu.VMEM((owned * block_rows, width), BF16),
            pltpu.VMEM(w_in.shape, BF16),
            pltpu.VMEM(w_out.shape, BF16),
            pltpu.VMEM((1, width), F32),
            pltpu.VMEM((1, width), F32),
            pltpu.VMEM((2,) + cand_ids.shape, jnp.int32),
            pltpu.VMEM(block_user.shape, jnp.int32),
            pltpu.VMEM((n, pair_rows, width), BF16),
            pltpu.VMEM((n, pair_rows, width), BF16),
            pltpu.VMEM((n, shard_rows, width), BF16),
            pltpu.VMEM((cands, width), BF16),
            pltpu.VMEM((cands, width), BF16),
            pltpu.VMEM((cands, width), F32),
            pltpu.VMEM((cands, width), BF16),
            pltpu.VMEM((n // 2 * pair_rows, width), BF16),
            pltpu.VMEM((cands, width), F32),
            pltpu.VMEM(pairs, BF16),
            pltpu.VMEM(pairs, BF16),
            dma((8,)),
            dma((n,)),
            dma((n,)),
            dma((bits,)),
            dma((bits,)),
            dma((HEADS // 2,)),
            dma((HEADS // 2,)),
            dma((2,)),
        ],
        compiler_params=pltpu.CompilerParams(
            collective_id=0, has_side_effects=True, vmem_limit_bytes=56 * 1024 * 1024
        ),
    )(
        history.reshape(-1, width), pool, cand_ids, block_user, norm_gain.reshape(1, -1),
        attn_gain.reshape(1, -1), w_in, w_out,
    )
    return out.reshape(users_here, per_user, width)


def solution(mesh):
    in_specs = (
        P(("parts", "wide"), None, None),
        P(("parts", "wide"), None),
        P(("parts", "wide"), None),
        P("parts", None),
        P(),
        P(),
        P(),
        P(),
    )
    out_specs = P(("parts", "wide"), None, None)
    return jax.shard_map(
        functools.partial(body, mesh.shape["wide"]), mesh=mesh, in_specs=in_specs,
        out_specs=out_specs, check_vma=False,
    )
```

time: 83.1 us -> 66.1 us (0.80)
  the two profiles are of different devices: /device:TPU:13 before, /device:TPU:0 now
where the time goes in v2:
time: 66.1 us; the launch traced here: 65.9 us
  Pallas kernels  64 us (97%)
  local copies, waits for them, and re-layouts  1.87 us (3%)
    pallas_call x1, Pallas kernels, body(): pl.pallas_call(functools.partial(kernel, n, users_here, per_user, block_r...  64 us
    unnamed x1, local copies, waits for them, and re-layouts  1.87 us

profile of v2, /device:TPU:0, one launch (start us, length us, event | category | flops | bytes accessed | tf_op | source)
XLA Modules:
  0.0 65.9 jit_solution(38419514010907473)
XLA Ops:
  0.0 64.0 %shard_map.82 = bf16[256,1024]{1,0:T(8,128)(2,1)} custom-call(bf16[512,1024]{1,0:T(8,128)(2,1)} %bitcast.5, bf16[16,1024]{1,0:T(8,128)(2,1)} %pool_hbm.1, s32[2,128]{1,0:T(2,128)} %ids_hbm.1, s32[16,64]{1,0:T(8,128)} %user_hbm.1, f32[1,1024]{1,0:T(1,128)} %bitcast.6, f32[1,1024]{1,0:T(1,128)} %bitcast.7, bf16[1024,4096]{1,0:T(8,128)(2,1)} %win_hbm.1, ...), custom_call_target="tpu_custom_call" | custom-call | tf_op jit(solution)/shard_map/pallas_call | solution.py:351
  64.0 1.9 %copy.10 = bf16[2,128,1024]{2,1,0:T(8,128)(2,1)} copy(bf16[2,128,1024]{2,1,0:T(8,128)(2,1)} %bitcast.4) | data formatting | bytes 1048576

commit v3 on v2

--- a/solution.py
+++ b/solution.py
@@ -136,42 +136,59 @@
         found = jnp.dot(chosen, hist[...], preferred_element_type=F32)
         sendb[pl.ds(first, count)] = found.reshape(count, pair_rows, width).astype(BF16)
 
-    def send_all(first, last, peer_shift, slot_shift):
-        def one(i, carry):
-            step = last - 1 - i
-            block_copy(step, step - peer_shift, step + slot_shift).start()
-            return carry
-
-        lax.fori_loop(0, last - first, one, 0)
-
+    def send(step, peer_shift, slot_shift):
+        block_copy(step, step - peer_shift, step + slot_shift).start()
+
+    pick(half, quarter)
+    pick(half + quarter, quarter)
     pl.semaphore_wait(barrier, n - 1)
     pool_copy(0).start()
     ids_copy.start()
-    pick(half + quarter, quarter)
+    pick(quarter, quarter)
     pool_copy(0).wait_recv()
     pool_copy(1).start()
-    pick(half, quarter)
-    pool_copy(1).wait_recv()
-    pool_copy(2).start()
 
     @pl.when(is_middle)
     def _():
         recvb[pl.ds(half, 1)] = sendb[pl.ds(half + quarter, 1)]
-        send_all(half + quarter + 1, n, half + quarter, -quarter)
-        send_all(half, half + quarter, 0, 0)
+
+        def one(i, carry):
+            send(half + i, 0, 0)
+            send(quarter + i, 0, 0)
+            return carry
+
+        def proxied(i, carry):
+            send(half + quarter + i, half + quarter, -quarter)
+            return carry
+
+        lax.fori_loop(1, quarter, proxied, 0)
+        lax.fori_loop(0, quarter, one, 0)
 
     @pl.when(jnp.logical_not(is_middle))
     def _():
-        send_all(half, half + quarter, quarter, quarter)
-        send_all(half + quarter, n, 0, 0)
-
-    pick(quarter, quarter)
-    for stage in range(3, bits):
+        def one(i, carry):
+            send(half + i, quarter, quarter)
+            send(half + quarter + i, 0, 0)
+            return carry
+
+        def near(i, carry):
+            send(quarter + i, 0, 0)
+            return carry
+
+        lax.fori_loop(0, quarter, one, 0)
+        lax.fori_loop(0, quarter, near, 0)
+
+    pick(0, quarter)
+    recvb[pl.ds(0, 1)] = sendb[pl.ds(0, 1)]
+    for stage in range(2, bits):
         pool_copy(stage - 1).wait_recv()
         pool_copy(stage).start()
-    pick(0, quarter)
-    send_all(1, half, 0, 0)
-    recvb[pl.ds(0, 1)] = sendb[pl.ds(0, 1)]
+
+    def plane(i, carry):
+        send(i, 0, 0)
+        return carry
+
+    lax.fori_loop(1, quarter, plane, 0)
     pool_copy(bits - 1).wait_recv()
 
     def event_users(ranker, first, flips_from):
@@ -382,7 +399,7 @@
             dma((2,)),
         ],
         compiler_params=pltpu.CompilerParams(
-            collective_id=0, has_side_effects=True, vmem_limit_bytes=56 * 1024 * 1024
+            collective_id=0, has_side_effects=True, vmem_limit_bytes=40 * 1024 * 1024
         ),
     )(
         history.reshape(-1, width), pool, cand_ids, block_user, norm_gain.reshape(1, -1),

time: 66.1 us -> 76.2 us (1.15)
  the two profiles are of different devices: /device:TPU:0 before, /device:TPU:25 now
where the time goes in v3:
time: 76.2 us; the launch traced here: 75.8 us
  Pallas kernels  65.3 us (86%)
  local copies, waits for them, and re-layouts  10.5 us (14%)
    pallas_call x1, Pallas kernels, body(): pl.pallas_call(functools.partial(kernel, n, users_here, per_user, block_r...  65.3 us
    unnamed x17, local copies, waits for them, and re-layouts  10.5 us

profile of v3, /device:TPU:25, one launch (start us, length us, event | category | flops | bytes accessed | tf_op | source)
XLA Modules:
  0.0 75.8 jit_solution(4179426663695332727)
XLA Ops:
  0.0 0.0 copy-start
  0.0 3.4 %copy-done = bf16[1024,4096]{1,0:T(8,128)(2,1)S(1)} copy-done((bf16[1024,4096]{1,0:T(8,128)(2,1)S(1)}, bf16[1024,4096]{1,0:T(8,128)(2,1)}, u32[]{:S(2)}) %copy-start) | copy-done | bytes 8388632
  3.4 0.0 copy-start.1
  3.4 1.6 %copy-done.1 = bf16[1024,1024]{1,0:T(8,128)(2,1)S(1)} copy-done((bf16[1024,1024]{1,0:T(8,128)(2,1)S(1)}, bf16[1024,1024]{1,0:T(8,128)(2,1)}, u32[]{:S(2)}) %copy-start.1) | copy-done | bytes 2097176
  5.0 0.0 copy-start.2
  5.0 1.2 %copy-done.2 = bf16[64,8,1024]{2,1,0:T(8,128)(2,1)S(1)} copy-done((bf16[64,8,1024]{2,1,0:T(8,128)(2,1)S(1)}, bf16[64,8,1024]{2,1,0:T(8,128)(2,1)}, u32[]{:S(2)}) %copy-start.2) | copy-done | bytes 1048600
  6.2 0.0 copy-start.3
  6.2 0.8 copy-done.3
  7.0 0.0 copy-start.4
  7.0 0.7 copy-done.4
  7.7 0.0 copy-start.5
  7.7 0.7 copy-done.5
  8.3 0.0 copy-start.6
  8.3 0.7 copy-done.6
  9.0 0.0 copy-start.7
  9.0 0.7 copy-done.7
  9.7 65.3 %shard_map.82 = bf16[256,1024]{1,0:T(8,128)(2,1)S(1)} custom-call(bf16[512,1024]{1,0:T(8,128)(2,1)S(1)} %bitcast.5, bf16[16,1024]{1,0:T(8,128)(2,1)S(1)} %copy-done.3, s32[2,128]{1,0:T(2,128)S(1)} %copy-done.7, s32[16,64]{1,0:T(8,128)S(1)} %copy-done.4, f32[1,1024]{1,0:T(1,128)S(1)} %bitcast.6, f32[1,1024]{1,0:T(1,128)S(1)} %bitcast.7, ...), custom_call_target="tpu_custom_call" | custom-call | tf_op jit(solution)/shard_map/pallas_call | solution.py:368
  75.0 0.8 %copy.10 = bf16[2,128,1024]{2,1,0:T(8,128)(2,1)} copy(bf16[2,128,1024]{2,1,0:T(8,128)(2,1)S(1)} %bitcast.4) | data formatting | bytes 1048576
Async XLA Ops:
  0.0 3.4 %copy-start = (bf16[1024,4096]{1,0:T(8,128)(2,1)S(1)}, bf16[1024,4096]{1,0:T(8,128)(2,1)}, u32[]{:S(2)}) copy-start(bf16[1024,4096]{1,0:T(8,128)(2,1)} %win_hbm.1) | copy-start | bytes 25165828
  3.4 1.6 %copy-start.1 = (bf16[1024,1024]{1,0:T(8,128)(2,1)S(1)}, bf16[1024,1024]{1,0:T(8,128)(2,1)}, u32[]{:S(2)}) copy-start(bf16[1024,1024]{1,0:T(8,128)(2,1)} %wout_hbm.1) | copy-start | bytes 6291460
  5.0 1.2 %copy-start.2 = (bf16[64,8,1024]{2,1,0:T(8,128)(2,1)S(1)}, bf16[64,8,1024]{2,1,0:T(8,128)(2,1)}, u32[]{:S(2)}) copy-start(bf16[64,8,1024]{2,1,0:T(8,128)(2,1)} %param.8) | copy-start | bytes 3145732
  6.2 0.8 %copy-start.3 = (bf16[16,1024]{1,0:T(8,128)(2,1)S(1)}, bf16[16,1024]{1,0:T(8,128)(2,1)}, u32[]{:S(2)}) copy-start(bf16[16,1024]{1,0:T(8,128)(2,1)} %pool_hbm.1) | copy-start | bytes 98308
  7.0 0.7 copy-start.4
  7.7 0.7 copy-start.5
  8.3 0.7 copy-start.6
  9.0 0.7 copy-start.7

commit v4 on v2

--- a/solution.py
+++ b/solution.py
@@ -8,6 +8,7 @@
 from jax.sharding import PartitionSpec as P
 
 HEADS = 8
+STEPS = 4
 F32 = jnp.float32
 BF16 = jnp.bfloat16
 
@@ -53,6 +54,7 @@
 ):
     bits = (n - 1).bit_length()
     half, quarter = n // 2, n // 4
+    unit = quarter // STEPS
     me = lax.axis_index("wide")
     middle = (me // half + me // quarter) % 2
     is_middle = middle == 1
@@ -136,63 +138,78 @@
         found = jnp.dot(chosen, hist[...], preferred_element_type=F32)
         sendb[pl.ds(first, count)] = found.reshape(count, pair_rows, width).astype(BF16)
 
-    def send_all(first, last, peer_shift, slot_shift):
+    def run(act, first, count, peer_shift=0, slot_shift=0):
         def one(i, carry):
-            step = last - 1 - i
-            block_copy(step, step - peer_shift, step + slot_shift).start()
+            copy = block_copy(first + i, first + i - peer_shift, first + i + slot_shift)
+            copy.start() if act else copy.wait_send()
             return carry
 
-        lax.fori_loop(0, last - first, one, 0)
-
+        lax.fori_loop(0, count, one, 0)
+
+    def end_step(i, act):
+        if i < STEPS // 2:
+            run(act, half + 2 * i * unit, 2 * unit, quarter, quarter)
+        run(act, half + quarter + i * unit, unit)
+        if i >= STEPS // 2:
+            run(act, quarter + (2 * i - STEPS) * unit, 2 * unit)
+
+    def middle_step(i, act):
+        run(act, half + i * unit, unit)
+        run(act, quarter + i * unit, unit)
+
+    def turn(step, i):
+        step(i - 1, False)
+        step(i, True)
+
+    pick(half, quarter)
+    pick(half + quarter, quarter)
     pl.semaphore_wait(barrier, n - 1)
     pool_copy(0).start()
     ids_copy.start()
-    pick(half + quarter, quarter)
+    pick(quarter, quarter)
     pool_copy(0).wait_recv()
     pool_copy(1).start()
-    pick(half, quarter)
-    pool_copy(1).wait_recv()
-    pool_copy(2).start()
 
     @pl.when(is_middle)
     def _():
         recvb[pl.ds(half, 1)] = sendb[pl.ds(half + quarter, 1)]
-        send_all(half + quarter + 1, n, half + quarter, -quarter)
-        send_all(half, half + quarter, 0, 0)
+
+        run(True, half + quarter + 1, quarter - 1, half + quarter, -quarter)
+        middle_step(0, True)
 
     @pl.when(jnp.logical_not(is_middle))
     def _():
-        send_all(half, half + quarter, quarter, quarter)
-        send_all(half + quarter, n, 0, 0)
-
-    pick(quarter, quarter)
-    for stage in range(3, bits):
+        end_step(0, True)
+
+    pick(0, quarter)
+    recvb[pl.ds(0, 1)] = sendb[pl.ds(0, 1)]
+    for stage in range(2, bits):
         pool_copy(stage - 1).wait_recv()
         pool_copy(stage).start()
-    pick(0, quarter)
-    send_all(1, half, 0, 0)
-    recvb[pl.ds(0, 1)] = sendb[pl.ds(0, 1)]
+
+    run(True, 1, quarter - 1)
     pool_copy(bits - 1).wait_recv()
 
-    def event_users(ranker, first, flips_from):
-        shape = (n, half * pair_rows)
+    def by_slot(ranker):
         arrived = targets == ranker
         count = exact_dot(jnp.where(arrived, 1.0, 0.0), jnp.where(earlier, 1.0, 0.0))
         count = count.astype(jnp.int32)
         label = users - ranker * users_here + 1
-        lanes = lane(shape)
-        slot_here = (lanes % pair_rows) // block_rows
-        owner = flip(me, lane((1, half * pair_rows)) // pair_rows + flips_from, bits)
+        return [
+            jnp.sum(jnp.where(arrived & (count == slot), label, 0), axis=1, keepdims=True)
+            for slot in range(slots)
+        ]
+
+    def by_event(table, blocks, step_of):
+        shape = (n, blocks * pair_rows)
+        slot_here = (lane(shape) % pair_rows) // block_rows
+        owner = flip(me, step_of(lane((1, shape[1])) // pair_rows), bits)
         total = jnp.zeros(shape, jnp.int32)
         for slot in range(slots):
-            at_slot = jnp.sum(
-                jnp.where(arrived & (count == slot), label, 0), axis=1, keepdims=True
-            )
-            total = total + jnp.where(slot_here == slot, at_slot, 0)
+            total = total + jnp.where(slot_here == slot, table[slot], 0)
         return jnp.sum(jnp.where(row(shape) == owner, total, 0), axis=0, keepdims=True) - 1
 
-    near_users = event_users(me, 0, 0)
-    far_users = event_users(jnp.where(is_middle, mate, me), half, half * (1 - middle))
+    own_table = by_slot(me)
 
     shards, shard_rows, _ = poolb.shape
     pool_rows = shards * shard_rows
@@ -229,9 +246,12 @@
 
         lax.fori_loop(0, HEADS // 2, one, 0)
 
-    def attend(first, count, query_ref, event_user, emit):
-        rows = count * pair_rows
-        hidden = recvb[pl.ds(first, count)].astype(F32).reshape(rows, width)
+    def attend(pieces, query_ref, event_user, emit):
+        rows = sum(count for _, count in pieces) * pair_rows
+        hidden = jnp.concatenate([
+            recvb[pl.ds(first, count)].astype(F32).reshape(count * pair_rows, width)
+            for first, count in pieces
+        ], axis=0)
         normed[pl.ds(0, rows)] = (normalize(hidden) * gain[...]).astype(BF16)
         mask = row((cands, rows)) // per_user == event_user
 
@@ -264,6 +284,19 @@
         acc[:, columns(j)] += value
 
     ids_copy.wait_recv()
+    found, normed_items = pool_items(0)
+    items[...] = found.astype(BF16)
+
+    def front(j):
+        gate[:, columns(j)] = project(normed_items, j, 0)
+        queries[:, columns(j)] = project(normed_items, j, width).astype(BF16)
+
+    each_pair(front)
+    acc[...] = jnp.zeros_like(acc)
+
+    def attend_plane():
+        arrive(1, quarter)
+        attend([(0, quarter)], queries, by_event(own_table, quarter, lambda b: b), add)
 
     @pl.when(is_middle)
     def _():
@@ -273,28 +306,24 @@
             mate_queries[:, columns(j)] = project(mate_items, j, width).astype(BF16)
 
         each_pair(ask)
+        far_users = by_event(by_slot(mate), half, lambda b: b)
+        for i in range(1, STEPS - 1):
+            turn(middle_step, i)
         arrive(half + 1, n)
 
         def emit(j, value):
             part_out[j] = value.astype(BF16)
             part_copy(j).start()
 
-        attend(half, half, mate_queries, far_users, emit)
-
-    found, normed_items = pool_items(0)
-    items[...] = found.astype(BF16)
-
-    def front(j):
-        gate[:, columns(j)] = project(normed_items, j, 0)
-        queries[:, columns(j)] = project(normed_items, j, width).astype(BF16)
-
-    each_pair(front)
-    acc[...] = jnp.zeros_like(acc)
-    arrive(1, half)
-    attend(0, half, queries, near_users, add)
-
-    @pl.when(is_middle)
-    def _():
+        attend([(half, half)], mate_queries, far_users, emit)
+        turn(middle_step, STEPS - 1)
+        attend_plane()
+        arrive(quarter, half)
+        attend(
+            [(quarter, quarter)], queries,
+            by_event(own_table, quarter, lambda b: b + quarter), add,
+        )
+
         def join(j):
             part_copy(j).wait_recv()
             add(j, part_in[j].astype(F32))
@@ -303,11 +332,19 @@
 
     @pl.when(jnp.logical_not(is_middle))
     def _():
-        for g in range(2):
-            first = half + g * quarter
-            arrive(first, first + quarter)
-            event_user = far_users[:, g * quarter * pair_rows:(g + 1) * quarter * pair_rows]
-            attend(first, quarter, queries, event_user, add)
+        for i in range(STEPS):
+            if i + 1 < STEPS:
+                turn(end_step, i + 1)
+            if i == 0:
+                attend_plane()
+            pieces = [(part * quarter + i * unit, unit) for part in range(1, 4)]
+            for first, count in pieces:
+                arrive(first, first + count)
+            event_user = by_event(
+                own_table, 3 * unit,
+                lambda b: quarter * (1 + b // unit) + i * unit + b % unit,
+            )
+            attend(pieces, queries, event_user, add)
 
     gated = (normalize(acc[...]) * again[...] * gate[...]).astype(BF16)
 
@@ -321,20 +358,17 @@
     for stage in range(bits):
         pool_copy(stage).wait_send()
 
-    def sent(step, carry):
-        block_copy(step, 1, step).wait_send()
-        return carry
-
-    lax.fori_loop(1, half + quarter, sent, 0)
-    lax.fori_loop(half + quarter + 1, n, sent, 0)
+    run(False, 1, quarter - 1)
+
+    @pl.when(is_middle)
+    def _():
+        run(False, half + quarter + 1, quarter - 1)
+        middle_step(STEPS - 1, False)
+        each_pair(lambda j: part_copy(j).wait_send())
 
     @pl.when(jnp.logical_not(is_middle))
     def _():
-        sent(half + quarter, 0)
-
-    @pl.when(is_middle)
-    def _():
-        each_pair(lambda j: part_copy(j).wait_send())
+        end_step(STEPS - 1, False)
 
 
 def body(n, history, pool, cand_ids, block_user, norm_gain, w_in, attn_gain, w_out):

time: 66.1 us -> 69.6 us (1.053)
  Pallas kernels: 64 us -> 67.6 us
    pallas_call x1, Pallas kernels: 64 us -> 67.6 us  [body(): pl.pallas_call(functools.partial(kernel, n, users_here, per_user, block_r...]
where the time goes in v4:
time: 69.6 us; the launch traced here: 69.4 us
  Pallas kernels  67.6 us (97%)
  local copies, waits for them, and re-layouts  1.87 us (3%)
    pallas_call x1, Pallas kernels, body(): pl.pallas_call(functools.partial(kernel, n, users_here, per_user, block_r...  67.6 us
    unnamed x1, local copies, waits for them, and re-layouts  1.87 us

profile of v4, /device:TPU:0, one launch (start us, length us, event | category | flops | bytes accessed | tf_op | source)
XLA Modules:
  0.0 69.4 jit_solution(3933285525661225479)
XLA Ops:
  0.0 67.6 %shard_map.82 = bf16[256,1024]{1,0:T(8,128)(2,1)} custom-call(bf16[512,1024]{1,0:T(8,128)(2,1)} %bitcast.5, bf16[16,1024]{1,0:T(8,128)(2,1)} %pool_hbm.1, s32[2,128]{1,0:T(2,128)} %ids_hbm.1, s32[16,64]{1,0:T(8,128)} %user_hbm.1, f32[1,1024]{1,0:T(1,128)} %bitcast.6, f32[1,1024]{1,0:T(1,128)} %bitcast.7, bf16[1024,4096]{1,0:T(8,128)(2,1)} %win_hbm.1, ...), custom_call_target="tpu_custom_call" | custom-call | tf_op jit(solution)/shard_map/pallas_call | solution.py:385
  67.6 1.9 %copy.10 = bf16[2,128,1024]{2,1,0:T(8,128)(2,1)} copy(bf16[2,128,1024]{2,1,0:T(8,128)(2,1)} %bitcast.4) | data formatting | bytes 1048576

commit v5 on v4

--- a/solution.py
+++ b/solution.py
@@ -8,13 +8,13 @@
 from jax.sharding import PartitionSpec as P
 
 HEADS = 8
-STEPS = 4
+STEPS = 2
 F32 = jnp.float32
 BF16 = jnp.bfloat16
 
 
-def silu(x):
-    half = 0.5 * x
+def silu(x, scale=1.0):
+    half = (0.5 * scale) * x
     return half + half * jnp.tanh(half)
 
 
@@ -154,8 +154,9 @@
             run(act, quarter + (2 * i - STEPS) * unit, 2 * unit)
 
     def middle_step(i, act):
+        if i == 0:
+            run(act, quarter, quarter)
         run(act, half + i * unit, unit)
-        run(act, quarter + i * unit, unit)
 
     def turn(step, i):
         step(i - 1, False)
@@ -239,12 +240,12 @@
     def project(rows_in, j, offset):
         return silu(jnp.dot(rows_in, win[:, columns(j, offset)], preferred_element_type=F32))
 
-    def each_pair(step):
+    def each_pair(step, unroll=1):
         def one(j, carry):
             step(j)
             return carry
 
-        lax.fori_loop(0, HEADS // 2, one, 0)
+        lax.fori_loop(0, HEADS // 2, one, 0, unroll=unroll)
 
     def attend(pieces, query_ref, event_user, emit):
         rows = sum(count for _, count in pieces) * pair_rows
@@ -267,11 +268,11 @@
                     query[:, part], keys[:, part], (((1,), (1,)), ((), ())),
                     preferred_element_type=F32,
                 )
-                weights = jnp.where(mask, silu(scores * head ** (-0.5)), 0.0).astype(BF16)
+                weights = jnp.where(mask, silu(scores, head ** (-0.5)), 0.0).astype(BF16)
                 parts.append(jnp.dot(weights, vals[:, part], preferred_element_type=F32))
             emit(j, jnp.concatenate(parts, axis=1))
 
-        each_pair(pair)
+        each_pair(pair, unroll=2)
 
     def arrive(first, last):
         def one(slot, carry):
@@ -298,6 +299,11 @@
         arrive(1, quarter)
         attend([(0, quarter)], queries, by_event(own_table, quarter, lambda b: b), add)
 
+    def attend_near():
+        arrive(quarter, half)
+        event_user = by_event(own_table, quarter, lambda b: b + quarter)
+        attend([(quarter, quarter)], queries, event_user, add)
+
     @pl.when(is_middle)
     def _():
         _, mate_items = pool_items(1)
@@ -307,7 +313,7 @@
 
         each_pair(ask)
         far_users = by_event(by_slot(mate), half, lambda b: b)
-        for i in range(1, STEPS - 1):
+        for i in range(1, STEPS):
             turn(middle_step, i)
         arrive(half + 1, n)
 
@@ -316,13 +322,8 @@
             part_copy(j).start()
 
         attend([(half, half)], mate_queries, far_users, emit)
-        turn(middle_step, STEPS - 1)
         attend_plane()
-        arrive(quarter, half)
-        attend(
-            [(quarter, quarter)], queries,
-            by_event(own_table, quarter, lambda b: b + quarter), add,
-        )
+        attend_near()
 
         def join(j):
             part_copy(j).wait_recv()
@@ -337,12 +338,13 @@
                 turn(end_step, i + 1)
             if i == 0:
                 attend_plane()
-            pieces = [(part * quarter + i * unit, unit) for part in range(1, 4)]
+                attend_near()
+            pieces = [(part * quarter + i * unit, unit) for part in range(2, 4)]
             for first, count in pieces:
                 arrive(first, first + count)
             event_user = by_event(
-                own_table, 3 * unit,
-                lambda b: quarter * (1 + b // unit) + i * unit + b % unit,
+                own_table, 2 * unit,
+                lambda b: quarter * (2 + b // unit) + i * unit + b % unit,
             )
             attend(pieces, queries, event_user, add)
 

time: 69.6 us -> 64.8 us (0.931)
  the two profiles are of different devices: /device:TPU:0 before, /device:TPU:10 now
where the time goes in v5:
time: 64.8 us; the launch traced here: 64.6 us
  Pallas kernels  62.7 us (97%)
  local copies, waits for them, and re-layouts  1.87 us (3%)
    pallas_call x1, Pallas kernels, body(): pl.pallas_call(functools.partial(kernel, n, users_here, per_user, block_r...  62.7 us
    unnamed x1, local copies, waits for them, and re-layouts  1.87 us

profile of v5, /device:TPU:10, one launch (start us, length us, event | category | flops | bytes accessed | tf_op | source)
XLA Modules:
  0.0 64.6 jit_solution(9328521912839744585)
XLA Ops:
  0.0 62.7 %shard_map.82 = bf16[256,1024]{1,0:T(8,128)(2,1)} custom-call(bf16[512,1024]{1,0:T(8,128)(2,1)} %bitcast.5, bf16[16,1024]{1,0:T(8,128)(2,1)} %pool_hbm.1, s32[2,128]{1,0:T(2,128)} %ids_hbm.1, s32[16,64]{1,0:T(8,128)} %user_hbm.1, f32[1,1024]{1,0:T(1,128)} %bitcast.6, f32[1,1024]{1,0:T(1,128)} %bitcast.7, bf16[1024,4096]{1,0:T(8,128)(2,1)} %win_hbm.1, ...), custom_call_target="tpu_custom_call" | custom-call | tf_op jit(solution)/shard_map/pallas_call | solution.py:387
  62.7 1.9 %copy.10 = bf16[2,128,1024]{2,1,0:T(8,128)(2,1)} copy(bf16[2,128,1024]{2,1,0:T(8,128)(2,1)} %bitcast.4) | data formatting | bytes 1048576

commit v6 on v5

--- a/solution.py
+++ b/solution.py
@@ -153,10 +153,8 @@
         if i >= STEPS // 2:
             run(act, quarter + (2 * i - STEPS) * unit, 2 * unit)
 
-    def middle_step(i, act):
-        if i == 0:
-            run(act, quarter, quarter)
-        run(act, half + i * unit, unit)
+    def middle_sends(act):
+        run(act, quarter, 2 * quarter)
 
     def turn(step, i):
         step(i - 1, False)
@@ -176,7 +174,7 @@
         recvb[pl.ds(half, 1)] = sendb[pl.ds(half + quarter, 1)]
 
         run(True, half + quarter + 1, quarter - 1, half + quarter, -quarter)
-        middle_step(0, True)
+        middle_sends(True)
 
     @pl.when(jnp.logical_not(is_middle))
     def _():
@@ -313,8 +311,6 @@
 
         each_pair(ask)
         far_users = by_event(by_slot(mate), half, lambda b: b)
-        for i in range(1, STEPS):
-            turn(middle_step, i)
         arrive(half + 1, n)
 
         def emit(j, value):
@@ -365,7 +361,7 @@
     @pl.when(is_middle)
     def _():
         run(False, half + quarter + 1, quarter - 1)
-        middle_step(STEPS - 1, False)
+        middle_sends(False)
         each_pair(lambda j: part_copy(j).wait_send())
 
     @pl.when(jnp.logical_not(is_middle))

time: 64.8 us -> 65.2 us (level)
  the two profiles are of different devices: /device:TPU:10 before, /device:TPU:0 now
where the time goes in v6:
time: 65.2 us; the launch traced here: 64.2 us
  Pallas kernels  62.4 us (96%)
  local copies, waits for them, and re-layouts  1.87 us (3%)
    pallas_call x1, Pallas kernels, body(): pl.pallas_call(functools.partial(kernel, n, users_here, per_user, block_r...  62.4 us
    unnamed x1, local copies, waits for them, and re-layouts  1.87 us

profile of v6, /device:TPU:0, one launch (start us, length us, event | category | flops | bytes accessed | tf_op | source)
XLA Modules:
  0.0 64.2 jit_solution(2242251165382160105)
XLA Ops:
  0.0 62.4 %shard_map.82 = bf16[256,1024]{1,0:T(8,128)(2,1)} custom-call(bf16[512,1024]{1,0:T(8,128)(2,1)} %bitcast.5, bf16[16,1024]{1,0:T(8,128)(2,1)} %pool_hbm.1, s32[2,128]{1,0:T(2,128)} %ids_hbm.1, s32[16,64]{1,0:T(8,128)} %user_hbm.1, f32[1,1024]{1,0:T(1,128)} %bitcast.6, f32[1,1024]{1,0:T(1,128)} %bitcast.7, bf16[1024,4096]{1,0:T(8,128)(2,1)} %win_hbm.1, ...), custom_call_target="tpu_custom_call" | custom-call | tf_op jit(solution)/shard_map/pallas_call | solution.py:383
  62.4 1.9 %copy.10 = bf16[2,128,1024]{2,1,0:T(8,128)(2,1)} copy(bf16[2,128,1024]{2,1,0:T(8,128)(2,1)} %bitcast.4) | data formatting | bytes 1048576
